TPU v7x, 256 devices: a whole 4x4x8 slice. The times are simulated.
256 devices in a mesh: bins: 8 (over y, core), sites: 32 (over x, z).
Axes of the slice: x: 4, y: 4, z: 8, core: 2. Of those that a mesh axis runs over, the one named last changes fastest.
Arguments:
- greens: bfloat16 [4096, 8, 2048], P('sites'), may hold values from -6 to 6
- moment_rate: bfloat16 [8, 64, 64], P('bins'), may hold values from -0.09375 to 0.09375
- bin_owner: int32 [256, 64, 1], P(('bins', 'sites')), may hold values from 0 to 31; in each aligned block of 64 rows (0 to 63, 64 to 127, ..., all dimensions but the last counted through in order) at most 3 rows name the same one
- bin_local: int32 [256, 64], P(('bins', 'sites')), may hold values from 0 to 127
Outputs:
- shaking: bfloat16 [256, 8, 8, 2048], P(('bins', 'sites'))
Inputs may be any that keep to these rules, and one draw needn't show every extreme that they name: `bin_owner`: among the 64 subfaults of one site no range number appears more than 3 times, and in some sites one appears exactly 3 times.
All inputs are finite; a program needn't handle non-finite values.
Results may differ from a plain program's by a relative error of at most 0.001.
Values may be sent and summed in bfloat16 or wider, within the bound.
A program may use at most 128 MiB of HBM per device.

v0:
```python
import jax
import jax.numpy as jnp
from jax import lax
from jax.sharding import PartitionSpec as P

TB = 32


def kernel_table(moment):
    variations, faults, duration = moment.shape
    offsets = duration // TB + 1
    lagged = (
        jnp.arange(offsets)[:, None, None] * TB
        + jnp.arange(TB)[None, None, :]
        - jnp.arange(TB)[None, :, None]
    )
    inside = (lagged >= 0) & (lagged < duration)
    picked = moment[:, :, jnp.clip(lagged, 0, duration - 1)]
    picked = jnp.where(inside, picked, jnp.zeros((), moment.dtype))
    return picked.transpose(2, 1, 3, 0, 4).reshape(offsets, faults, TB, variations * TB)


def stack_blocks(fetched, offsets):
    leading = fetched.ndim - 3
    faults, channels, samples = fetched.shape[leading:]
    block_count = samples // TB
    blocks = fetched.reshape(fetched.shape[:leading] + (faults, channels, block_count, TB))
    permuted = tuple(range(leading)) + (leading + 1, leading + 2, leading, leading + 3)
    blocks = jnp.transpose(blocks, permuted)
    widths = [(0, 0)] * leading + [(0, 0), (offsets - 1, 0), (0, 0), (0, 0)]
    padded = jnp.pad(blocks, widths)
    return jnp.stack(
        [
            lax.slice_in_dim(
                padded, offsets - 1 - offset, offsets - 1 - offset + block_count, axis=leading + 1
            )
            for offset in range(offsets)
        ]
    )


def pick_rows(greens, wanted):
    present = wanted >= 0
    fetched = greens[jnp.maximum(wanted, 0)]
    return jnp.where(present[..., None, None], fetched, jnp.zeros((), greens.dtype))


def local(greens, moment_rate, bin_owner, bin_local):
    full_rate = lax.all_gather(moment_rate, "bins", axis=0, tiled=True)
    toeplitz = kernel_table(full_rate)
    owners = bin_owner[:, :, 0]
    sites_here, fault_count = owners.shape
    peer_count = lax.axis_size("sites")
    capacity = 3 * fault_count // (2 * peer_count)
    onehot = (owners[:, :, None] == jnp.arange(peer_count, dtype=jnp.int32)[None, None, :]).astype(
        jnp.int32
    )
    slot_rank = jnp.sum((jnp.cumsum(onehot, axis=1) - 1) * onehot, axis=2)
    site_index = jnp.broadcast_to(jnp.arange(sites_here, dtype=jnp.int32)[:, None], owners.shape)
    fault_index = jnp.arange(fault_count, dtype=jnp.int32)[None, :]
    empty_slots = jnp.full((peer_count, sites_here, capacity), -1, jnp.int32)
    requested = empty_slots.at[owners, site_index, slot_rank].set(bin_local)
    channels = greens.shape[1]
    samples = greens.shape[2]
    faults_sent = empty_slots.at[owners, site_index, slot_rank].set(fault_index)
    wanted = lax.all_to_all(requested, "sites", split_axis=0, concat_axis=0, tiled=True)
    faults = lax.all_to_all(faults_sent, "sites", split_axis=0, concat_axis=0, tiled=True)
    fetched = pick_rows(greens, wanted)
    kernels = toeplitz[:, jnp.maximum(faults, 0)]
    shifted = stack_blocks(fetched, toeplitz.shape[0])
    partial_value = jnp.einsum(
        "opicnsj,opisjy->picny", shifted, kernels, preferred_element_type=jnp.float32
    )
    returned = lax.all_to_all(partial_value, "sites", split_axis=0, concat_axis=0, tiled=True)
    summed = jnp.sum(returned, axis=0)
    variations = full_rate.shape[0]
    traces = summed.reshape(sites_here, channels, samples // TB, variations, TB)
    traces = traces.transpose(0, 3, 1, 2, 4).reshape(sites_here, variations, channels, samples)
    return traces.astype(jnp.bfloat16)


def solution(mesh):
    placed = (
        P("sites", None, None),
        P("bins", None, None),
        P(("bins", "sites"), None, None),
        P(("bins", "sites"), None),
    )
    return jax.shard_map(
        local,
        mesh=mesh,
        in_specs=placed,
        out_specs=P(("bins", "sites"), None, None, None),
        check_vma=False,
    )
```

profile of v0, /device:TPU:8, one launch (start us, length us, event | category | flops | bytes accessed | tf_op | source)
XLA Modules:
  0.0 542.6 jit_solution(14788933037740882837)
XLA Ops:
  0.7 0.7 fusion.12
  1.5 0.8 select_reduce_fusion
  2.4 5.8 %scatter_fusion = s32[32,3]{0,1:T(4,128)S(1)} fusion(s32[32,3]{0,1:T(4,128)S(1)} %broadcast.240.clone.1, s32[64]{0:T(128)S(1)} %fusion.14, s32[64]{0:T(128)} %bitcast.68), kind=kCustom, calls=%fused_computation.3 | custom fusion | bytes 1280 | tf_op jit(solution)/shard_map/scatter | solution.py:62
  8.1 0.7 copy.32
  8.8 11.3 %all-to-all-start = ((s32[32,1,3]{2,1,0:T(1,128)}), s32[32,1,3]{2,1,0:T(1,128)S(1)}, u32[]{:S(2)}, u32[]{:S(2)}) async-start(s32[32,1,3]{2,1,0:T(1,128)} %copy.32), calls=%async_computation | async-start | bytes 32768 | tf_op jit(solution)/shard_map/all_to_all | solution.py:66
  20.4 13.2 %all_gather.3 = bf16[8,64,64]{2,1,0:T(8,128)(2,1)S(1)} all-gather(bf16[1,64,64]{2,1,0:T(8,128)(2,1)} %param.5), channel_id=1, replica_groups=mesh['bins'=8,'sites'=32] {'bins'}, dimensions={0}, use_global_device_ids=true | all-gather | bytes 73728 | tf_op jit(solution)/shard_map/all_gather | solution.py:49
  33.7 21.7 %gather_fusion.1 = bf16[3072,8,64]{2,1,0:T(8,128)(2,1)} fusion(bf16[8,64,64]{1,0,2:T(8,128)(2,1)S(1)} %copy.38, s32[3072]{0:T(1024)S(1)} %broadcast_clamp_fusion), kind=kCustom, calls=%fused_computation.1 | custom fusion | bytes 6303744 | tf_op jit(solution)/shard_map/gather | solution.py:18
  55.4 6.6 %select_bitcast_fusion = bf16[3,64,32,8,32]{1,3,4,2,0:T(8,128)(2,1)} fusion(bf16[3,32,32,8,64]{4,3,2,1,0:T(8,128)(2,1)} %bitcast.61, pred[3,32,32]{2,1,0:T(8,128)(4,1)S(1)} %fusion.11), kind=kLoop, calls=%fused_computation.13 | loop fusion | flops 1572864 | bytes 6294528 | tf_op jit(solution)/shard_map/jit(_where)/select_n | solution.py:19
  62.0 3.5 scatter_fusion.1
  65.5 0.7 copy.40
  66.2 7.5 %copy.39 = bf16[3,64,32,8,32]{1,4,3,2,0:T(8,128)(2,1)} copy(bf16[3,64,32,8,32]{1,3,4,2,0:T(8,128)(2,1)} %select_bitcast_fusion) | data formatting | bytes 6291456 | tf_op jit(solution)/shard_map/jit(_where)/select_n | solution.py:19
  73.7 7.9 %copy.41 = bf16[3,64,32,256]{3,2,0,1:T(8,128)(2,1)} copy(bf16[3,64,32,256]{1,3,2,0:T(8,128)(2,1)} %bitcast.62) | data formatting | bytes 6291456 | tf_op jit(solution)/shard_map/reshape | solution.py:20
  81.6 10.0 %all-to-all-start.1 = ((s32[32,1,3]{2,1,0:T(1,128)}), s32[32,1,3]{2,1,0:T(1,128)S(1)}, u32[]{:S(2)}, u32[]{:S(2)}) async-start(s32[32,1,3]{2,1,0:T(1,128)} %copy.40), calls=%async_computation.1 | async-start | bytes 32768 | tf_op jit(solution)/shard_map/all_to_all | solution.py:67
  91.7 9.4 %all-to-all-done.1 = s32[32,1,3]{2,1,0:T(1,128)S(1)} async-done(((s32[32,1,3]{2,1,0:T(1,128)}), s32[32,1,3]{2,1,0:T(1,128)S(1)}, u32[]{:S(2)}, u32[]{:S(2)}) %all-to-all-start.1) | async-done | bytes 416 | tf_op jit(solution)/shard_map/all_to_all | solution.py:67
  101.6 3.0 gather_fusion
  104.5 11.6 %gather.12 = bf16[32,1,3,8,64,32]{5,4,3,2,0,1:T(8,128)(2,1)} reshape(bf16[96,8,2048]{2,1,0:T(8,128)(2,1)S(1)} %gather_fusion) | data formatting | bytes 6291456 | tf_op jit(solution)/shard_map/gather | solution.py:44
  116.2 12.3 %copy.35 = bf16[32,1,3,8,64,32]{4,5,2,3,0,1:T(8,128)(2,1)} copy(bf16[32,1,3,8,64,32]{5,4,3,2,0,1:T(8,128)(2,1)} %gather.12) | data formatting | bytes 6291456 | tf_op jit(solution)/shard_map/gather | solution.py:44
  128.5 6.3 %fusion.6 = (bf16[1,32,1,8,64,3,32]{4,6,5,0,3,1,2:T(8,128)(2,1)}, bf16[32,1,8,64,3,32]{3,5,4,2,0,1:T(8,128)(2,1)S(1)}) fusion(bf16[32,1,3,8,64,32]{4,5,2,3,0,1:T(8,128)(2,1)} %copy.35, pred[32,3]{1,0:T(8,128)(4,1)S(1)} %copy.34), kind=kLoop, calls=%fused_computation.17 | loop fusion | flops 1572864 | bytes 9437280 | tf_op jit(solution)/shard_map/stack | solution.py:32
  134.8 6.8 %slice_bitcast_fusion.1 = (bf16[1,32,1,8,64,3,32]{4,6,5,0,3,1,2:T(8,128)(2,1)}, bf16[1,32,1,8,64,3,32]{4,6,5,0,3,1,2:T(8,128)(2,1)}) fusion(bf16[32,1,8,64,3,32]{3,5,4,2,0,1:T(8,128)(2,1)S(1)} %get-tuple-element.6), kind=kLoop, calls=%fused_computation.15 | loop fusion | bytes 9437184 | tf_op jit(solution)/shard_map/stack | solution.py:32
  141.5 5.1 gather_fusion.2
  146.6 15.5 %fusion.5 = f32[32,1,8,64,256]{4,3,2,1,0:T(8,128)} fusion(bf16[1,32,1,8,64,3,32]{4,6,5,0,3,1,2:T(8,128)(2,1)} %get-tuple-element.8, bf16[1,32,1,8,64,3,32]{4,6,5,0,3,1,2:T(8,128)(2,1)} %get-tuple-element.7, bf16[1,32,1,8,64,3,32]{4,6,5,0,3,1,2:T(8,128)(2,1)} %get-tuple-element.5, bf16[3,32,3,32,256,1]{4,3,0,2,1,5:T(8,128)(2,1)} %bitcast.63), kind=kOutput, calls=%fused_computation.12 | convolution fusion | flops 2425356288 | bytes 30932992 | tf_op jit(solution)/shard_map/opicnsj,opisjy->picny/dot_general | solution.py:71
  162.1 370.3 %all_to_all.15 = f32[32,1,8,64,256]{4,3,2,1,0:T(8,128)} all-to-all(f32[32,1,8,64,256]{4,3,2,1,0:T(8,128)} %fusion.5), channel_id=1, replica_groups=mesh['bins'=8,'sites'=32] {'sites'}, dimensions={0} | all-to-all | bytes 33554432 | tf_op jit(solution)/shard_map/all_to_all | solution.py:74
  532.5 7.5 %bitcast_reduce_fusion = bf16[8,64,256]{2,1,0:T(8,128)(2,1)S(1)} fusion(f32[32,1,8,64,256]{4,3,2,1,0:T(8,128)} %all_to_all.15), kind=kLoop, calls=%fused_computation.11 | loop fusion | flops 4063232 | bytes 17039360 | tf_op jit(solution)/shard_map/reduce_sum | solution.py:75
  540.7 1.8 convert_element_type.37
  (27 shorter events, 2.4 us)
Async XLA Ops:
  8.8 72.8 %all-to-all-start = ((s32[32,1,3]{2,1,0:T(1,128)}), s32[32,1,3]{2,1,0:T(1,128)S(1)}, u32[]{:S(2)}, u32[]{:S(2)}) async-start(s32[32,1,3]{2,1,0:T(1,128)} %copy.32), calls=%async_computation | async-start | bytes 32768 | tf_op jit(solution)/shard_map/all_to_all | solution.py:66
  81.6 19.5 %all-to-all-start.1 = ((s32[32,1,3]{2,1,0:T(1,128)}), s32[32,1,3]{2,1,0:T(1,128)S(1)}, u32[]{:S(2)}, u32[]{:S(2)}) async-start(s32[32,1,3]{2,1,0:T(1,128)} %copy.40), calls=%async_computation.1 | async-start | bytes 32768 | tf_op jit(solution)/shard_map/all_to_all | solution.py:67
where the time goes:
time: 543 us
  blocking collectives  383 us (71%)
  local copies, waits for them, and re-layouts  89.7 us (17%)
  other arithmetic  23 us (4%)
  starting transfers between devices  21.3 us (4%)
  matrix products  15.5 us (3%)
  waiting for transfers between devices  9.4 us (2%)
    all_to_all x1, blocking collectives, local(): lax.all_to_all(partial_value, 'sites', split_axis=0, concat_axis=0, tiled...  370 us
    gather x3, local copies, waits for them, and re-layouts, pick_rows(): fetched = greens[jnp.maximum(wanted, 0)]  26.9 us
    gather x1, local copies, waits for them, and re-layouts, kernel_table(): picked = moment[:, :, jnp.clip(lagged, 0, duration - 1)]  21.7 us
    dot_general x1, matrix products, local(): jnp.einsum('opicnsj,opisjy->picny', shifted, kernels, preferred_element_t...  15.5 us
    all_gather x1, blocking collectives, local(): full_rate = lax.all_gather(moment_rate, 'bins', axis=0, tiled=True)  13.2 us
    all_to_all x1, starting transfers between devices, local(): lax.all_to_all(requested, 'sites', split_axis=0, concat_axis=0, tiled=True)  11.3 us
  transfers between devices with their start and end apart: 2, of which 1 were waited for; matrix products, arithmetic and copies ran while one was open for 9% of the time, Pallas kernels for 0%

commit v1 on v0

v1 whole, which is shorter than its diff:
```python
import functools
import jax
import jax.numpy as jnp
from jax import lax
from jax.experimental import pallas as pl
from jax.experimental.pallas import tpu as pltpu
from jax.sharding import PartitionSpec as P

MESH = pl.DeviceIdType.MESH
NX, NZ = 4, 8
NXZ = NX * NZ
CAP = 3
HALF = 64
LANES = 128
LEVELS = 2


def plan():
    jobs = [s * k for k in range(LEVELS, 0, -1) for s in (1, -1)] + [0]
    groups = {job: [] for job in jobs}
    for dz in (4, 3, -3, 2, -2, 1, -1, 0):
        for dx in (2, 1, 3, 0):
            sign = (1 if dx in (0, 1) else -1) if dz == 4 else (1 if dz > 0 else -1)
            far = sign * abs(dz)
            hop = sign * max(abs(dz) - LEVELS, 0)
            groups[far - hop].append((dx, dz, hop))
    order, spans = [], {}
    for job in jobs:
        spans[job] = (len(order), len(order) + len(groups[job]))
        order += groups[job]
    sends = []
    for k in range(LEVELS, 0, -1):
        for pair in zip(groups[k], groups[-k]):
            sends += pair
    sends += groups[0]
    return jobs, order, spans, [order.index(g) for g in sends]


def kernel(
    greens, moment, owner, local_bin, out,
    rows, land, sent, toep, base, moments, moment_out, table_out, tables, table_smem,
    left, acc, inbox,
    rows_sem, smem_sem, table_send, table_recv, moment_send, moment_recv, row_send, row_recv, sum_send, sum_recv,
):
    jobs, order, spans, send_order = plan()
    bins = lax.axis_index("bins")
    site = lax.axis_index("sites")
    x, z = site // NZ, site % NZ
    nbins = moments.shape[0]

    def at(px, pz):
        return (px + NX) % NX * NZ + (pz + NZ) % NZ

    def table_copy(step):
        other = (site + step) % NXZ
        return pltpu.make_async_remote_copy(
            table_out, tables.at[site], table_send.at[step - 1], table_recv.at[step - 1],
            device_id=(bins, other), device_id_type=MESH,
        )

    def moment_copy(step):
        other = (bins + step) % nbins
        return pltpu.make_async_remote_copy(
            moment_out, moments.at[bins], moment_send.at[step - 1], moment_recv.at[step - 1],
            device_id=(other, site), device_id_type=MESH,
        )

    def row_copy(g):
        dx, dz, hop = order[g]
        return pltpu.make_async_remote_copy(
            sent.at[pl.ds(CAP * g, CAP)], land.at[pl.ds(CAP * g, CAP)], row_send.at[g], row_recv.at[g],
            device_id=(bins, at(x + dx, z + hop)), device_id_type=MESH,
        )

    def box(job):
        return 0 if job > 0 else 1, abs(job) - 1

    def sum_copy(job, p):
        side, level = box(job)
        index = (side * LEVELS + level) * 4 + p
        return pltpu.make_async_remote_copy(
            acc.at[jobs.index(job), p], inbox.at[side, level, p], sum_send.at[index], sum_recv.at[index],
            device_id=(bins, at(x, z + (1 if job > 0 else -1))), device_id_type=MESH,
        )

    fetch = pltpu.make_async_copy(greens, rows, rows_sem)
    fetch.start()

    barrier = pltpu.get_barrier_semaphore()

    @pl.loop(1, NXZ)
    def _(step):
        pl.semaphore_signal(barrier, inc=1, device_id=(bins, (site + step) % NXZ), device_id_type=MESH)

    @pl.loop(1, nbins)
    def _(step):
        pl.semaphore_signal(barrier, inc=1, device_id=((bins + step) % nbins, site), device_id_type=MESH)

    faults = owner.shape[1]
    fault = lax.broadcasted_iota(jnp.int32, (faults, LANES), 0)
    hit = owner[0] == lax.broadcasted_iota(jnp.int32, (faults, LANES), 1)
    rank = hit.astype(jnp.int32)
    shift = 1
    while shift < faults:
        rank += jnp.concatenate([jnp.zeros((shift, LANES), jnp.int32), rank[:-shift]], axis=0)
        shift *= 2
    square = (faults, faults)
    diagonal = lax.broadcasted_iota(jnp.int32, square, 0) == lax.broadcasted_iota(jnp.int32, square, 1)
    wanted = jnp.sum(jnp.where(diagonal, local_bin[...] + 1, 0), axis=1, keepdims=True)
    lines = []
    for r in range(CAP):
        here = hit & (rank == r + 1)
        lines.append(jnp.sum(jnp.where(here, wanted, 0), axis=0, keepdims=True))
        lines.append(jnp.sum(jnp.where(here, fault + 1, 0), axis=0, keepdims=True))
    table = jnp.concatenate(lines + [jnp.zeros((8 - 2 * CAP, LANES), jnp.int32)], axis=0)
    table_out[...] = table
    tables[site] = table
    own_rate = jnp.concatenate([moment[0], jnp.zeros((faults, HALF), jnp.bfloat16)], axis=1)
    moment_out[...] = own_rate
    moments[bins] = own_rate

    pl.semaphore_wait(barrier, NXZ - 1 + nbins - 1)

    @pl.loop(1, NXZ)
    def _(step):
        table_copy(step).start()

    @pl.loop(1, nbins)
    def _(step):
        moment_copy(step).start()

    acc[...] = jnp.zeros_like(acc)

    @pl.loop(1, NXZ)
    def _(step):
        table_copy(step).wait_recv()

    to_smem = pltpu.make_async_copy(tables, table_smem, smem_sem)
    to_smem.start()
    to_smem.wait()
    fetch.wait()

    for g in send_order:
        dx, dz, hop = order[g]
        here = dx == 0 and hop == 0
        asking = at(x + dx, z + dz)
        target = land if here else sent

        def gather(r, _, g=g, asking=asking, target=target):
            row = rows[jnp.maximum(table_smem[asking, 2 * r, site] - 1, 0)]
            target[CAP * g + r] = jnp.concatenate(
                [row[:, LANES * m : LANES * (m + 1)] for m in range(row.shape[1] // LANES)], axis=0
            )
            return 0

        lax.fori_loop(0, CAP, gather, 0)
        if not here:
            row_copy(g).start()

    for g, (dx, dz, hop) in enumerate(order):
        asking = at(x, z - hop + dz)
        source = at(x - dx, z - hop)
        for r in range(CAP):
            left[CAP * g + r] = table_smem[asking, 2 * r + 1, source]

    @pl.loop(1, nbins)
    def _(step):
        moment_copy(step).wait_recv()

    for p in range(4):
        base[p] = moments[2 * p + 1].astype(jnp.float32) + pltpu.roll(
            moments[2 * p].astype(jnp.float32), HALF, 1
        )
    lane = lax.broadcasted_iota(jnp.int32, (LANES, LANES), 1)
    lag = lane - lax.broadcasted_iota(jnp.int32, (LANES, LANES), 0)
    inside = ((lane < HALF) & (lag < 0) & (lag >= -HALF)) | ((lane >= HALF) & (lag >= 0) & (lag < HALF))
    toep[0] = jnp.zeros(toep.shape[1:], toep.dtype)

    @pl.loop(0, faults)
    def _(f):
        for p in range(4):
            spread = jnp.broadcast_to(base[p, pl.ds(f, 1), :], (LANES, LANES))
            turned = pltpu.roll(spread, 0, 1, stride=1, stride_axis=0)
            toep[f + 1, :, LANES * p : LANES * (p + 1)] = jnp.where(inside, turned, 0.0).astype(jnp.bfloat16)

    def window(slot):
        now = land[slot]
        swapped = pltpu.roll(now.astype(jnp.float32), HALF, 1)
        before = jnp.concatenate([jnp.zeros((8, LANES), jnp.float32), swapped[:-8]], axis=0)
        early = jnp.where(lane < HALF, before, swapped)
        return jnp.concatenate([early.astype(jnp.bfloat16), now], axis=0)

    def add_groups(job):
        first, last = spans[job]
        for g in range(first, last):
            dx, dz, hop = order[g]
            if dx != 0 or hop != 0:
                row_copy(g).wait_recv()

        def pair(i, _):
            slot = CAP * first + 2 * i
            a = jnp.concatenate([window(slot), window(slot + 1)], axis=1)
            b = jnp.concatenate([toep[left[slot]], toep[left[slot + 1]]], axis=0)
            c = jnp.dot(a, b, preferred_element_type=jnp.float32)
            for p in range(4):
                acc[jobs.index(job), p] += c[:, LANES * p : LANES * (p + 1)]
            return 0

        lax.fori_loop(0, CAP * (last - first) // 2, pair, 0)

    for job in jobs:
        add_groups(job)
        if job == 0:
            continue
        for p in range(4):
            if abs(job) < LEVELS:
                further = job + (1 if job > 0 else -1)
                sum_copy(further, p).wait_recv()
                side, level = box(further)
                acc[jobs.index(job), p] += inbox[side, level, p]
            sum_copy(job, p).start()

    half = lax.broadcasted_iota(jnp.int32, (8, LANES), 1) < HALF
    for p in range(4):
        total = acc[jobs.index(0), p]
        if LEVELS > 0:
            for job in (1, -1):
                sum_copy(job, p).wait_recv()
                side, level = box(job)
                total = total + inbox[side, level, p]
        for m in range(LANES // 8):
            early = total[8 * m : 8 * m + 8]
            late = total[LANES + 8 * m : LANES + 8 * m + 8]
            where = slice(LANES * m, LANES * (m + 1))
            out[0, 2 * p, :, where] = jnp.where(half, early, pltpu.roll(late, HALF, 1)).astype(out.dtype)
            out[0, 2 * p + 1, :, where] = jnp.where(half, pltpu.roll(early, HALF, 1), late).astype(out.dtype)

    @pl.loop(1, NXZ)
    def _(step):
        table_copy(step).wait_send()

    @pl.loop(1, nbins)
    def _(step):
        moment_copy(step).wait_send()

    for g, (dx, dz, hop) in enumerate(order):
        if dx != 0 or hop != 0:
            row_copy(g).wait_send()
    for job in jobs:
        if job != 0:
            for p in range(4):
                sum_copy(job, p).wait_send()


def local(greens, moment_rate, bin_owner, bin_local):
    bins, channels, samples = greens.shape
    nbins = lax.axis_size("bins")
    faults = moment_rate.shape[1]
    slots = NXZ * CAP
    vmem, dma = pltpu.VMEM, pltpu.SemaphoreType.DMA
    sums = 2 * LEVELS + 1
    return pl.pallas_call(
        kernel,
        out_shape=jax.ShapeDtypeStruct((1, nbins, channels, samples), jnp.bfloat16),
        in_specs=[
            pl.BlockSpec(memory_space=pl.ANY),
            pl.BlockSpec(memory_space=vmem),
            pl.BlockSpec(memory_space=vmem),
            pl.BlockSpec(memory_space=vmem),
        ],
        out_specs=pl.BlockSpec(memory_space=vmem),
        scratch_shapes=[
            vmem((bins, channels, samples), jnp.bfloat16),
            vmem((slots, LANES, LANES), jnp.bfloat16),
            vmem((slots, LANES, LANES), jnp.bfloat16),
            vmem((faults + 1, LANES, 4 * LANES), jnp.bfloat16),
            vmem((4, faults, LANES), jnp.float32),
            vmem((nbins, faults, LANES), jnp.bfloat16),
            vmem((faults, LANES), jnp.bfloat16),
            vmem((8, LANES), jnp.int32),
            vmem((NXZ, 8, LANES), jnp.int32),
            pltpu.SMEM((NXZ, 8, LANES), jnp.int32),
            pltpu.SMEM((slots,), jnp.int32),
            vmem((sums, 4, 2 * LANES, LANES), jnp.float32),
            vmem((2, max(LEVELS, 1), 4, 2 * LANES, LANES), jnp.float32),
            dma,
            dma,
            dma((NXZ - 1,)),
            dma((NXZ - 1,)),
            dma((nbins - 1,)),
            dma((nbins - 1,)),
            dma((NXZ,)),
            dma((NXZ,)),
            dma((8 * max(LEVELS, 1),)),
            dma((8 * max(LEVELS, 1),)),
        ],
        compiler_params=pltpu.CompilerParams(
            collective_id=0, has_side_effects=True, vmem_limit_bytes=48 * 2**20
        ),
        cost_estimate=pl.CostEstimate(
            flops=slots * 2 * 256 * 128 * 512, bytes_accessed=2 * greens.size, transcendentals=0
        ),
    )(greens, moment_rate, bin_owner, bin_local)


def solution(mesh):
    placed = (
        P("sites", None, None),
        P("bins", None, None),
        P(("bins", "sites"), None, None),
        P(("bins", "sites"), None),
    )
    return jax.shard_map(
        local,
        mesh=mesh,
        in_specs=placed,
        out_specs=P(("bins", "sites"), None, None, None),
        check_vma=False,
    )
```

time: 543 us -> 78.9 us (0.15)
  blocking collectives: 383 us -> 0 us
  local copies, waits for them, and re-layouts: 89.7 us -> 5.01 us
  Pallas kernels: 0 us -> 73.6 us
  other arithmetic: 23 us -> 0 us
  starting transfers between devices: 21.3 us -> 0 us
  matrix products: 15.5 us -> 0 us
  waiting for transfers between devices: 9.4 us -> 0 us
    all_to_all x1 -> x0, blocking collectives: 370 us -> none  [local(): lax.all_to_all(partial_value, 'sites', split_axis=0, concat_axis=0, tiled...]
    pallas_call x0 -> x1, Pallas kernels: none -> 73.6 us  [local(): pl.pallas_call(kernel, out_shape=jax.ShapeDtypeStruct((1, nbins, channels...]
    gather x5 -> x0, local copies, waits for them, and re-layouts: 53.7 us -> none  [the longest x3 26.9 us: pick_rows(): fetched = greens[jnp.maximum(wanted, 0)]]
    all_to_all x2 -> x0, starting transfers between devices: 21.3 us -> none  [the longest x1 11.3 us: local(): lax.all_to_all(requested, 'sites', split_axis=0, concat_axis=0, tiled=True)]
    dot_general x1 -> x0, matrix products: 15.5 us -> none  [local(): jnp.einsum('opicnsj,opisjy->picny', shifted, kernels, preferred_element_t...]
    all_gather x1 -> x0, blocking collectives: 13.2 us -> none  [local(): full_rate = lax.all_gather(moment_rate, 'bins', axis=0, tiled=True)]
    scatter x4 -> x0, local copies, waits for them, and re-layouts: 10.6 us -> none  [the longest x2 6.44 us: local(): requested = empty_slots.at[owners, site_index, slot_rank].set(bin_local)]
    all_to_all x2 -> x0, waiting for transfers between devices: 9.4 us -> none  [the longest x1 9.4 us: local(): lax.all_to_all(faults_sent, 'sites', split_axis=0, concat_axis=0, tiled=T...]
  transfers between devices with their start and end apart: 2 -> 0, of which waited for: 1 -> 0; matrix products, arithmetic and copies ran while one was open for 9% -> 0% of each run, Pallas kernels for 0% -> 0%
where the time goes in v1:
time: 78.9 us; the launch traced here: 78.7 us
  Pallas kernels  73.6 us (93%)
  local copies, waits for them, and re-layouts  5.01 us (6%)
    pallas_call x1, Pallas kernels, local(): pl.pallas_call(kernel, out_shape=jax.ShapeDtypeStruct((1, nbins, channels...  73.6 us
    unnamed x8, local copies, waits for them, and re-layouts  5.01 us

profile of v1, /device:TPU:8, one launch (start us, length us, event | category | flops | bytes accessed | tf_op | source)
XLA Modules:
  0.0 78.7 jit_solution(16950120906077993598)
XLA Ops:
  0.0 0.7 copy.5.owner
  0.7 0.0 copy-start
  0.7 2.2 %copy-done = bf16[128,8,2048]{2,1,0:T(8,128)(2,1)S(1)} copy-done((bf16[128,8,2048]{2,1,0:T(8,128)(2,1)S(1)}, bf16[128,8,2048]{2,1,0:T(8,128)(2,1)}, u32[]{:S(2)}) %copy-start) | copy-done | bytes 4194328
  2.9 0.0 copy-start.1
  2.9 0.7 copy-done.1
  3.7 0.0 copy-start.2
  3.7 0.7 copy-done.2
  4.3 73.6 %shard_map.46 = bf16[1,8,8,2048]{3,2,1,0:T(8,128)(2,1)S(1)} custom-call(bf16[128,8,2048]{2,1,0:T(8,128)(2,1)S(1)} %copy-done, bf16[1,64,64]{2,1,0:T(8,128)(2,1)S(1)} %copy-done.1, s32[1,64,1]{2,1,0:T(8,128)S(1)} %copy.5.owner, s32[1,64]{1,0:T(1,128)S(1)} %copy-done.2), custom_call_target="tpu_custom_call" | custom-call | flops 3221225472 | bytes 4194304 | tf_op jit(solution)/shard_map/pallas_call | solution.py:262
  78.0 0.7 copy.7
Async XLA Ops:
  0.7 2.2 %copy-start = (bf16[128,8,2048]{2,1,0:T(8,128)(2,1)S(1)}, bf16[128,8,2048]{2,1,0:T(8,128)(2,1)}, u32[]{:S(2)}) copy-start(bf16[128,8,2048]{2,1,0:T(8,128)(2,1)} %greens.1) | copy-start | bytes 12582916
  2.9 0.7 copy-start.1
  3.7 0.7 copy-start.2

commit v2 on v1

v2 whole, which is shorter than its diff:
```python
import functools
import jax
import jax.numpy as jnp
from jax import lax
from jax.experimental import pallas as pl
from jax.experimental.pallas import tpu as pltpu
from jax.sharding import PartitionSpec as P

MESH = pl.DeviceIdType.MESH
NX, NZ = 4, 8
NXZ = NX * NZ
CAP = 3
HALF = 64
LANES = 128
LEVELS = 2
PARTS = 2


def plan():
    jobs = [s * k for k in range(LEVELS, 0, -1) for s in (1, -1)] + [0]
    groups = {job: [] for job in jobs}
    for dz in (4, 3, -3, 2, -2, 1, -1, 0):
        for dx in (2, 1, 3, 0):
            sign = (1 if dx in (0, 1) else -1) if dz == 4 else (1 if dz > 0 else -1)
            far = sign * abs(dz)
            hop = sign * max(abs(dz) - LEVELS, 0)
            groups[far - hop].append((dx, dz, hop))
    order, spans = [], {}
    for job in jobs:
        spans[job] = (len(order), len(order) + len(groups[job]))
        order += groups[job]
    ordered = []
    for k in range(LEVELS, 0, -1):
        ordered.append([g for pair in zip(groups[k], groups[-k]) for g in pair])
    ordered.append(groups[0])
    sends = []
    for h in range(PARTS):
        sends += [(h, order.index(g)) for level in ordered[:-1] for g in level]
    for h in range(PARTS):
        sends += [(h, order.index(g)) for g in ordered[-1]]
    return jobs, order, spans, sends


def kernel(
    greens_hbm, moment_hbm, owner_hbm, bin_hbm, out,
    moment, owner, local_bin, rows, land, sent, toep, base, moments, moment_out, table_out, tables, table_smem,
    left, windows, acc, inbox,
    fetch_sem, smem_sem, table_sem, moment_sem, row_send, row_recv, sum_send, sum_recv,
):
    jobs, order, spans, sends = plan()
    bins = lax.axis_index("bins")
    site = lax.axis_index("sites")
    x, z = site // NZ, site % NZ
    nbins = moments.shape[0]
    part = land.shape[2]

    def at(px, pz):
        return (px + NX) % NX * NZ + (pz + NZ) % NZ

    def table_copy(step):
        return pltpu.make_async_remote_copy(
            table_out, tables.at[site], table_sem.at[0], table_sem.at[1],
            device_id=(bins, (site + step) % NXZ), device_id_type=MESH,
        )

    def moment_copy(step):
        return pltpu.make_async_remote_copy(
            moment_out, moments.at[bins], moment_sem.at[0], moment_sem.at[1],
            device_id=((bins + step) % nbins, site), device_id_type=MESH,
        )

    def all_tables(sem):
        some = tables.at[pl.ds(0, NXZ - 1)]
        return pltpu.make_async_copy(some, some, sem)

    def all_moments(sem):
        some = moments.at[pl.ds(0, nbins - 1)]
        return pltpu.make_async_copy(some, some, sem)

    def row_copy(h, g):
        dx, dz, hop = order[g]
        return pltpu.make_async_remote_copy(
            sent.at[h, pl.ds(CAP * g, CAP)], land.at[h, pl.ds(CAP * g, CAP)], row_send.at[h, g], row_recv.at[h, g],
            device_id=(bins, at(x + dx, z + hop)), device_id_type=MESH,
        )

    def stays(g):
        return order[g][0] == 0 and order[g][2] == 0

    def box(job):
        return 0 if job > 0 else 1, abs(job) - 1

    def sum_copy(h, job, p):
        side, level = box(job)
        index = ((h * 2 + side) * LEVELS + level) * 4 + p
        return pltpu.make_async_remote_copy(
            acc.at[h, jobs.index(job), p], inbox.at[h, side, level, p], sum_send.at[index], sum_recv.at[index],
            device_id=(bins, at(x, z + (1 if job > 0 else -1))), device_id_type=MESH,
        )

    barrier = pltpu.get_barrier_semaphore()
    for step in range(1, NXZ):
        pl.semaphore_signal(barrier, inc=1, device_id=(bins, (site + step) % NXZ), device_id_type=MESH)
    for step in range(1, nbins):
        pl.semaphore_signal(barrier, inc=1, device_id=((bins + step) % nbins, site), device_id_type=MESH)

    fetches = [
        pltpu.make_async_copy(there, here, fetch_sem.at[i])
        for i, (there, here) in enumerate(
            ((owner_hbm, owner), (bin_hbm, local_bin), (moment_hbm, moment), (greens_hbm, rows))
        )
    ]
    for fetch in fetches:
        fetch.start()

    for fetch in fetches[:3]:
        fetch.wait()
    faults = owner.shape[1]
    fault = lax.broadcasted_iota(jnp.int32, (faults, LANES), 0)
    spot = lax.broadcasted_iota(jnp.int32, (faults, LANES), 1)
    square = (faults, faults)
    diagonal = lax.broadcasted_iota(jnp.int32, square, 0) == lax.broadcasted_iota(jnp.int32, square, 1)
    serving = jnp.sum(jnp.where(diagonal, owner[...], 0), axis=1, keepdims=True)
    wanted = jnp.sum(jnp.where(diagonal, local_bin[...] + 1, 0), axis=1, keepdims=True)
    hit = serving == spot % NXZ
    rank = hit.astype(jnp.int32)
    shift = 1
    while shift < faults:
        rank += jnp.concatenate([jnp.zeros((shift, LANES), jnp.int32), rank[:-shift]], axis=0)
        shift *= 2
    chosen = hit & (rank == spot // NXZ + 1)
    table = jnp.sum(jnp.where(chosen, wanted * 65536 + fault + 1, 0), axis=0, keepdims=True)
    table_out[...] = table
    tables[site] = table
    own_rate = jnp.concatenate([moment[0], jnp.zeros((faults, HALF), jnp.bfloat16)], axis=1)
    moment_out[...] = own_rate
    moments[bins] = own_rate

    pl.semaphore_wait(barrier, NXZ - 1 + nbins - 1)
    for step in range(1, NXZ):
        table_copy(step).start()
    all_tables(table_sem.at[1]).wait()
    to_smem = pltpu.make_async_copy(tables, table_smem, smem_sem)
    to_smem.start()
    to_smem.wait()
    fetches[3].wait()

    def pass_on(h, g):
        dx, dz, hop = order[g]
        asking = at(x + dx, z + dz)
        target = land if stays(g) else sent
        samples = part // 8 * LANES

        def gather(r, _):
            row = rows[jnp.maximum(table_smem[asking, 0, NXZ * r + site] // 65536 - 1, 0)]
            row = row[:, samples * h : samples * (h + 1)]
            target[h, CAP * g + r] = jnp.concatenate(
                [row[:, LANES * m : LANES * (m + 1)] for m in range(part // 8)], axis=0
            )
            return 0

        lax.fori_loop(0, CAP, gather, 0)
        if not stays(g):
            row_copy(h, g).start()

    for i, (h, g) in enumerate(sends):
        pass_on(h, g)
        if i == 8:
            for step in range(1, nbins):
                moment_copy(step).start()

    for g, (dx, dz, hop) in enumerate(order):
        asking = at(x, z - hop + dz)
        source = at(x - dx, z - hop)
        for r in range(CAP):
            left[CAP * g + r] = table_smem[asking, 0, NXZ * r + source] % 65536

    all_moments(moment_sem.at[1]).wait()
    for p in range(4):
        base[p] = moments[2 * p + 1].astype(jnp.float32) + pltpu.roll(
            moments[2 * p].astype(jnp.float32), HALF, 1
        )
    square = (LANES, LANES)
    lane = lax.broadcasted_iota(jnp.int32, square, 1)
    lag = lane - lax.broadcasted_iota(jnp.int32, square, 0)
    inside = ((lane < HALF) & (lag < 0) & (lag >= -HALF)) | ((lane >= HALF) & (lag >= 0) & (lag < HALF))
    toep[0] = jnp.zeros(toep.shape[1:], toep.dtype)

    @pl.loop(0, faults)
    def _(f):
        for p in range(4):
            spread = jnp.broadcast_to(base[p, pl.ds(f, 1), :], square)
            turned = pltpu.roll(spread, 0, 1, stride=1, stride_axis=0)
            toep[f + 1, :, LANES * p : LANES * (p + 1)] = jnp.where(inside, turned, 0.0).astype(jnp.bfloat16)

    early_lane = lax.broadcasted_iota(jnp.int32, (part, LANES), 1) < HALF

    def window(h, slot):
        now = land[h, slot]
        swapped = pltpu.roll(now.astype(jnp.float32), HALF, 1)
        if h == 0:
            edge = jnp.zeros((8, LANES), jnp.float32)
        else:
            edge = pltpu.roll(land[h - 1, slot].astype(jnp.float32)[part - 8 :], HALF, 1)
        before = jnp.concatenate([edge, swapped[: part - 8]], axis=0)
        return jnp.concatenate([jnp.where(early_lane, before, swapped).astype(jnp.bfloat16), now], axis=0)

    def own_sums(h, job):
        first, last = spans[job]
        size = min(last - first, 5)
        for start in range(first, last, size):
            for g in range(start, start + size):
                if not stays(g):
                    row_copy(h, g).wait_recv()
            slots = range(CAP * start, CAP * (start + size))
            for i, slot in enumerate(slots):
                windows[:, LANES * i : LANES * (i + 1)] = window(h, slot)
            tiles = jnp.concatenate([toep[left[slot]] for slot in slots], axis=0)
            c = jnp.dot(windows[:, : LANES * len(slots)], tiles, preferred_element_type=jnp.float32)
            for p in range(4):
                mine = c[:, LANES * p : LANES * (p + 1)]
                if start == first:
                    acc[h, jobs.index(job), p] = mine
                else:
                    acc[h, jobs.index(job), p] += mine

    def send_sums(h, job):
        for p in range(4):
            if abs(job) < LEVELS:
                further = job + (1 if job > 0 else -1)
                sum_copy(h, further, p).wait_recv()
                side, level = box(further)
                acc[h, jobs.index(job), p] += inbox[h, side, level, p]
            sum_copy(h, job, p).start()

    half = lax.broadcasted_iota(jnp.int32, (8, LANES), 1) < HALF

    def finish(h):
        for p in range(4):
            total = acc[h, jobs.index(0), p]
            for job in (1, -1):
                sum_copy(h, job, p).wait_recv()
                side, level = box(job)
                total = total + inbox[h, side, level, p]
            for m in range(part // 8):
                early = total[8 * m : 8 * m + 8]
                late = total[part + 8 * m : part + 8 * m + 8]
                start = part // 8 * LANES * h + LANES * m
                where = slice(start, start + LANES)
                out[0, 2 * p, :, where] = jnp.where(half, early, pltpu.roll(late, HALF, 1)).astype(out.dtype)
                out[0, 2 * p + 1, :, where] = jnp.where(half, pltpu.roll(early, HALF, 1), late).astype(out.dtype)

    for h in range(PARTS):
        for k in range(LEVELS, 0, -1):
            if k == 1 and h > 0:
                own_sums(h - 1, 0)
            for job in (k, -k):
                own_sums(h, job)
                if k == LEVELS:
                    send_sums(h, job)
            if k < LEVELS:
                for job in (k, -k):
                    send_sums(h, job)
    own_sums(PARTS - 1, 0)
    for h in range(PARTS):
        finish(h)

    all_tables(table_sem.at[0]).wait()
    all_moments(moment_sem.at[0]).wait()
    for h in range(PARTS):
        for g in range(len(order)):
            if not stays(g):
                row_copy(h, g).wait_send()
        for job in jobs:
            if job != 0:
                for p in range(4):
                    sum_copy(h, job, p).wait_send()


def local(greens, moment_rate, bin_owner, bin_local):
    bins, channels, samples = greens.shape
    nbins = lax.axis_size("bins")
    faults = moment_rate.shape[1]
    slots = NXZ * CAP
    part = samples // LANES * channels // PARTS
    vmem, dma = pltpu.VMEM, pltpu.SemaphoreType.DMA
    sums = 2 * LEVELS + 1
    return pl.pallas_call(
        kernel,
        out_shape=jax.ShapeDtypeStruct((1, nbins, channels, samples), jnp.bfloat16),
        in_specs=[pl.BlockSpec(memory_space=pltpu.HBM)] * 4,
        out_specs=pl.BlockSpec(memory_space=vmem),
        scratch_shapes=[
            vmem(moment_rate.shape, jnp.bfloat16),
            vmem(bin_local.shape, jnp.int32),
            vmem(bin_local.shape, jnp.int32),
            vmem((bins, channels, samples), jnp.bfloat16),
            vmem((PARTS, slots, part, LANES), jnp.bfloat16),
            vmem((PARTS, slots, part, LANES), jnp.bfloat16),
            vmem((faults + 1, LANES, 4 * LANES), jnp.bfloat16),
            vmem((4, faults, LANES), jnp.float32),
            vmem((nbins, faults, LANES), jnp.bfloat16),
            vmem((faults, LANES), jnp.bfloat16),
            vmem((1, LANES), jnp.int32),
            vmem((NXZ, 1, LANES), jnp.int32),
            pltpu.SMEM((NXZ, 1, LANES), jnp.int32),
            pltpu.SMEM((slots,), jnp.int32),
            vmem((2 * part, 5 * CAP * LANES), jnp.bfloat16),
            vmem((PARTS, sums, 4, 2 * part, LANES), jnp.float32),
            vmem((PARTS, 2, LEVELS, 4, 2 * part, LANES), jnp.float32),
            dma((4,)),
            dma,
            dma((2,)),
            dma((2,)),
            dma((PARTS, NXZ)),
            dma((PARTS, NXZ)),
            dma((PARTS * LEVELS * 8,)),
            dma((PARTS * LEVELS * 8,)),
        ],
        compiler_params=pltpu.CompilerParams(
            collective_id=0, has_side_effects=True, vmem_limit_bytes=64 * 2**20
        ),
        cost_estimate=pl.CostEstimate(
            flops=slots * 2 * 256 * 128 * 512, bytes_accessed=2 * greens.size, transcendentals=0
        ),
    )(greens, moment_rate, bin_owner.reshape(bin_local.shape), bin_local)


def solution(mesh):
    placed = (
        P("sites", None, None),
        P("bins", None, None),
        P(("bins", "sites"), None, None),
        P(("bins", "sites"), None),
    )
    return jax.shard_map(
        local,
        mesh=mesh,
        in_specs=placed,
        out_specs=P(("bins", "sites"), None, None, None),
        check_vma=False,
    )
```

time: 78.9 us -> 64.1 us (0.81)
  Pallas kernels: 73.6 us -> 62.3 us
  local copies, waits for them, and re-layouts: 5.01 us -> 1.67 us
    pallas_call x1, Pallas kernels: 73.6 us -> 62.3 us  [local(): pl.pallas_call(kernel, out_shape=jax.ShapeDtypeStruct((1, nbins, channels...]
    unnamed x8 -> x1, local copies, waits for them, and re-layouts: 5.01 us -> 1.67 us
where the time goes in v2:
time: 64.1 us; the launch traced here: 64 us
  Pallas kernels  62.3 us (97%)
  local copies, waits for them, and re-layouts  1.67 us (3%)
    pallas_call x1, Pallas kernels, local(): pl.pallas_call(kernel, out_shape=jax.ShapeDtypeStruct((1, nbins, channels...  62.3 us
    unnamed x1, local copies, waits for them, and re-layouts  1.67 us

profile of v2, /device:TPU:8, one launch (start us, length us, event | category | flops | bytes accessed | tf_op | source)
XLA Modules:
  0.0 64.0 jit_solution(10022165857100799997)
XLA Ops:
  0.0 62.3 %shard_map.46 = bf16[1,8,8,2048]{3,2,1,0:T(8,128)(2,1)} custom-call(bf16[128,8,2048]{2,1,0:T(8,128)(2,1)} %greens_hbm.1, bf16[1,64,64]{2,1,0:T(8,128)(2,1)} %moment_hbm.1, s32[1,64]{1,0:T(1,128)} %bitcast.1, s32[1,64]{1,0:T(1,128)} %bin_hbm.1), custom_call_target="tpu_custom_call" | custom-call | flops 3221225472 | bytes 4194304 | tf_op jit(solution)/shard_map/pallas_call | solution.py:288
  62.4 1.7 %copy.6 = bf16[1,8,8,2048]{3,2,1,0:T(8,128)(2,1)} copy(bf16[1,8,8,2048]{3,2,1,0:T(8,128)(2,1)} %shard_map.46) | data formatting | bytes 524288

commit v3 on v2

--- a/solution.py
+++ b/solution.py
@@ -19,8 +19,8 @@
 def plan():
     jobs = [s * k for k in range(LEVELS, 0, -1) for s in (1, -1)] + [0]
     groups = {job: [] for job in jobs}
-    for dz in (4, 3, -3, 2, -2, 1, -1, 0):
-        for dx in (2, 1, 3, 0):
+    for dz in (2, -2, 3, -3, 4, 1, -1, 0):
+        for dx in (1, 2, 3, 0):
             sign = (1 if dx in (0, 1) else -1) if dz == 4 else (1 if dz > 0 else -1)
             far = sign * abs(dz)
             hop = sign * max(abs(dz) - LEVELS, 0)

time: 64.1 us -> 62.4 us (0.973)
  Pallas kernels: 62.3 us -> 60.5 us
    pallas_call x1, Pallas kernels: 62.3 us -> 60.5 us  [local(): pl.pallas_call(kernel, out_shape=jax.ShapeDtypeStruct((1, nbins, channels...]
where the time goes in v3:
time: 62.4 us; the launch traced here: 62.1 us
  Pallas kernels  60.5 us (97%)
  local copies, waits for them, and re-layouts  1.67 us (3%)
    pallas_call x1, Pallas kernels, local(): pl.pallas_call(kernel, out_shape=jax.ShapeDtypeStruct((1, nbins, channels...  60.5 us
    unnamed x1, local copies, waits for them, and re-layouts  1.67 us

profile of v3, /device:TPU:8, one launch (start us, length us, event | category | flops | bytes accessed | tf_op | source)
XLA Modules:
  0.0 62.1 jit_solution(4515099507730636141)
XLA Ops:
  0.0 60.5 %shard_map.46 = bf16[1,8,8,2048]{3,2,1,0:T(8,128)(2,1)} custom-call(bf16[128,8,2048]{2,1,0:T(8,128)(2,1)} %greens_hbm.1, bf16[1,64,64]{2,1,0:T(8,128)(2,1)} %moment_hbm.1, s32[1,64]{1,0:T(1,128)} %bitcast.1, s32[1,64]{1,0:T(1,128)} %bin_hbm.1), custom_call_target="tpu_custom_call" | custom-call | flops 3221225472 | bytes 4194304 | tf_op jit(solution)/shard_map/pallas_call | solution.py:288
  60.5 1.7 %copy.6 = bf16[1,8,8,2048]{3,2,1,0:T(8,128)(2,1)} copy(bf16[1,8,8,2048]{3,2,1,0:T(8,128)(2,1)} %shard_map.46) | data formatting | bytes 524288

commit v4 on v3

--- a/solution.py
+++ b/solution.py
@@ -20,7 +20,7 @@
     jobs = [s * k for k in range(LEVELS, 0, -1) for s in (1, -1)] + [0]
     groups = {job: [] for job in jobs}
     for dz in (2, -2, 3, -3, 4, 1, -1, 0):
-        for dx in (1, 2, 3, 0):
+        for dx in (1, 3, 2, 0):
             sign = (1 if dx in (0, 1) else -1) if dz == 4 else (1 if dz > 0 else -1)
             far = sign * abs(dz)
             hop = sign * max(abs(dz) - LEVELS, 0)

time: 62.4 us -> 62.2 us (level)
  no operation moved by 1% of the time
where the time goes in v4:
time: 62.2 us; the launch traced here: 62.1 us
  Pallas kernels  60.5 us (97%)
  local copies, waits for them, and re-layouts  1.67 us (3%)
    pallas_call x1, Pallas kernels, local(): pl.pallas_call(kernel, out_shape=jax.ShapeDtypeStruct((1, nbins, channels...  60.5 us
    unnamed x1, local copies, waits for them, and re-layouts  1.67 us

profile of v4, /device:TPU:8, one launch (start us, length us, event | category | flops | bytes accessed | tf_op | source)
XLA Modules:
  0.0 62.1 jit_solution(9672346609348149366)
XLA Ops:
  0.0 60.5 %shard_map.46 = bf16[1,8,8,2048]{3,2,1,0:T(8,128)(2,1)} custom-call(bf16[128,8,2048]{2,1,0:T(8,128)(2,1)} %greens_hbm.1, bf16[1,64,64]{2,1,0:T(8,128)(2,1)} %moment_hbm.1, s32[1,64]{1,0:T(1,128)} %bitcast.1, s32[1,64]{1,0:T(1,128)} %bin_hbm.1), custom_call_target="tpu_custom_call" | custom-call | flops 3221225472 | bytes 4194304 | tf_op jit(solution)/shard_map/pallas_call | solution.py:288
  60.5 1.7 %copy.6 = bf16[1,8,8,2048]{3,2,1,0:T(8,128)(2,1)} copy(bf16[1,8,8,2048]{3,2,1,0:T(8,128)(2,1)} %shard_map.46) | data formatting | bytes 524288
